TPU v7x, 32 devices: a whole 2x2x4 slice. The times are simulated.
32 devices in a mesh: seq: 4 (over y, x), dec: 8 (over z, core).
Axes of the slice: x: 2, y: 2, z: 4, core: 2. Of those that a mesh axis runs over, the one named last changes fastest.
Arguments:
- latents: bfloat16 [4, 4, 12, 8, 1024], P('seq', None, None, 'dec'), may hold values from -6 to 6
- cache_lat: bfloat16 [4, 4, 12, 8, 512], P('seq', None, None, 'dec'), may hold values from -6 to 6
- cache_act: bfloat16 [4, 4, 12, 8, 12288], P('seq', None, None, 'dec'), may hold values from -0.25 to 2
- w_in: bfloat16 [27, 16, 384], replicated, may hold values from -0.3125 to 0.3125
- w_mid: bfloat16 [27, 384, 384], replicated, may hold values from -0.0625 to 0.0625
- norm_gain: float32 [384], replicated, may hold values from 0.1 to 1.9
- clip_group: int32 [4, 4], replicated, may hold values from 0 to 3, as said below
- band_rows: int32 [4, 8], replicated, may hold values from 2 to 96, as said below
Outputs:
- decoded: bfloat16 [4, 8, 96, 4, 16, 384], P('seq', 'dec')
Inputs may be any that keep to these rules, and one draw needn't show every extreme that they name: For every sequence shard s, clip_group[s, :] names each of the 4 groups once. Each row of band_rows sums to 384; every band has 2 rows or more, and in each row one band has exactly 96 rows.
All inputs are finite; a program needn't handle non-finite values.
Results may differ from a plain program's by a relative error of at most 0.0029.
Values may be sent and summed in bfloat16 or wider, within the bound.
No kernel may reach another device: no remote copies, remote signals or barrier semaphores. Data moves between devices by JAX's collectives and lax.ppermute only.
A program may use at most 384 MiB of HBM per device.

v0:
```python
import functools

import jax
import jax.numpy as jnp
from jax import lax
from jax.experimental import pallas as pl
from jax.experimental.pallas import tpu as pltpu
from jax.sharding import PartitionSpec as P

F = 4
CT = 2
COLS = 16
LANES = 128
EPSILON = 1e-06
F32 = jnp.float32
BF16 = jnp.bfloat16


def band_start(bands, group, owner, owners):
    total = jnp.int32(0)
    for other in range(owners):
        total = total + jnp.where(other < owner, bands[group, other], 0)
    return total


def first_unit(start, margin, source, owners, units, capacity):
    unit = (start - margin - source + owners - 1 + 2 * owners) // owners - 2
    return jnp.clip(unit, 0, units - capacity)


def clip_of(groups_ref, shard, group, clips):
    found = jnp.int32(0)
    for clip in range(clips):
        found = found + jnp.where(groups_ref[shard, clip] == group, clip, 0)
    return found


def pack_clips(groups_ref, lat_in, old_in, act_in, *refs, per_owner, per_step, clips):
    *outs, lat_ref, old_ref, act_ref, lat_scratch, act_scratch, sems = refs
    shard = lax.axis_index("seq")
    copies = [
        pltpu.make_async_copy(lat_in, lat_ref, sems.at[0]),
        pltpu.make_async_copy(old_in, old_ref, sems.at[1]),
    ]
    steps = per_owner // per_step
    for step in range(steps):
        rows = pl.ds(step * per_step, per_step)
        copies.append(
            pltpu.make_async_copy(act_in.at[rows], act_ref.at[rows], sems.at[2 + step])
        )
    for copy in copies:
        copy.start()
    chosen = [clip_of(groups_ref, shard, shard ^ other, clips) for other in range(clips)]
    tiles = act_ref.shape[2] // LANES
    depth = tiles // (CT * COLS)
    size = per_step * tiles
    lat_rows = outs[0].shape[0] - per_owner * tiles
    copies[0].wait()
    copies[1].wait()
    for row in range(per_owner):
        for frame in range(CT + F):
            for half in range(2):
                if frame < CT:
                    tile = frame * 2 + half
                    value = old_ref[row, :, tile * LANES : (tile + 1) * LANES]
                else:
                    tile = (frame - CT) * 2 + half
                    value = lat_ref[row, :, tile * LANES : (tile + 1) * LANES]
                at = row * 12 + half * (CT + F) + frame
                lat_scratch[pl.ds(at, clips, stride=lat_rows), :] = value.astype(F32)
    for out, clip in zip(outs, chosen):
        rows = pl.ds(pl.multiple_of(clip * lat_rows, 8), lat_rows)
        out[per_owner * tiles :, :] = lat_scratch[rows, :].astype(BF16)
    for step in range(steps):
        copies[2 + step].wait()
        for row in range(per_step):
            for frame in range(CT):
                for col in range(COLS):
                    for part in range(depth):
                        tile = (frame * COLS + col) * depth + part
                        at = row * tiles + (frame * depth + part) * COLS + col
                        value = act_ref[
                            step * per_step + row, :, tile * LANES : (tile + 1) * LANES
                        ]
                        act_scratch[step % 2, pl.ds(at, clips, stride=size), :] = value.astype(F32)
        for out, clip in zip(outs, chosen):
            rows = pl.ds(pl.multiple_of(clip * size, 8), size)
            out[step * size : (step + 1) * size, :] = act_scratch[step % 2, rows, :].astype(BF16)


def slice_latents(bands, *refs, owners, units, capacity, per_owner, cache_rows):
    *ins, out_ref, scratch = refs
    group = lax.axis_index("seq")
    source = lax.axis_index("dec")
    rows = out_ref.shape[1]
    size = per_owner * 12
    for other, in_ref in enumerate(ins):
        value = in_ref[cache_rows : cache_rows + size, :].astype(F32)
        scratch[pl.ds((group ^ other) * size, size), :] = value
    value = pltpu.roll(scratch[: units * 12, :], 64, 1)
    lane = lax.broadcasted_iota(jnp.int32, value.shape, 1)
    for width in (32, 16):
        up, down = pltpu.roll(value, width, 1), pltpu.roll(value, LANES - width, 1)
        value = jnp.where(lane & width == 0, down, up)
    scratch[: units * 12, :] = value
    for owner in range(owners):
        start = band_start(bands, group, owner, owners)
        unit = first_unit(start, 2, source, owners, units, capacity)
        out_ref[owner] = scratch[pl.ds(unit * 12, rows), :].astype(BF16)


def slice_caches(bands, *refs, owners, units, capacity, tiles):
    *ins, out_ref, scratch, in_sems, sems = refs
    group = lax.axis_index("seq")
    source = lax.axis_index("dec")
    size = scratch.shape[0] // len(ins)
    copies = []
    for other, in_ref in enumerate(ins):
        into = scratch.at[pl.ds(pl.multiple_of((group ^ other) * size, 16), size)]
        copies.append(pltpu.make_async_copy(in_ref.at[pl.ds(0, size)], into, in_sems.at[other]))
    for copy in copies:
        copy.start()
    for copy in copies:
        copy.wait()
    copies = []
    for owner in range(owners):
        start = band_start(bands, group, owner, owners)
        unit = first_unit(start, 1, source, owners, units, capacity)
        copies.append(
            pltpu.make_async_copy(
                scratch.at[pl.ds(pl.multiple_of(unit * tiles, 16), capacity * tiles)],
                out_ref.at[owner],
                sems.at[owner],
            )
        )
    for copy in copies:
        copy.start()
    for copy in copies:
        copy.wait()


def shift_columns(sums, width):
    rows = sums.shape[0]
    col = lax.rem(lax.broadcasted_iota(jnp.int32, (rows, width), 0), COLS)
    left = pltpu.roll(sums[:, :width], 1, 0)
    right = pltpu.roll(sums[:, 2 * width :], rows - 1, 0)
    total = sums[:, width : 2 * width] + jnp.where(col > 0, left, 0.0)
    return total + jnp.where(col < COLS - 1, right, 0.0)


def weight_copies(mid_ref, weights, sems, channels):
    copies = []
    for tap in range(27):
        into = weights.at[
            pl.ds(tap // 3 * channels, channels), pl.ds(tap % 3 * channels, channels)
        ]
        copies.append(pltpu.make_async_copy(mid_ref.at[tap], into, sems.at[tap]))
    return copies


def new_frames(
    bands, lat_ref, win_ref, gain_ref, mid_ref, out_ref, part_out, early_ref, weights,
    table, xs, windows_a, windows_b, first_a, first_b, act_a, act_b, late, part_ref,
    sems, out_sems, part_sems, early_sem,
    *, owners, units, capacity, height, block, band_max, channels,
):
    group = lax.axis_index("seq")
    owner = lax.axis_index("dec")
    live = bands[group, owner]
    start = band_start(bands, group, owner, owners)
    edge = lax.rem(height - lax.rem(start - 1 + height, height), height)
    blocks = band_max // block
    size = F * COLS
    per_source = lat_ref.shape[1]
    copies = weight_copies(mid_ref, weights, sems, channels)
    for copy in copies:
        copy.start()
    table[...] = jnp.zeros(table.shape, BF16)
    for time_tap in range(3):
        for row_tap in range(3):
            for col_tap in range(3):
                into = row_tap * 2 * LANES + (0, 64, LANES)[time_tap]
                into += ((0, 112, 96), (0, -16, -32), (0, 112, 96))[time_tap][col_tap]
                table[pl.ds(into, 16), :] = win_ref[time_tap * 9 + row_tap * 3 + col_tap]
    for source in range(owners):
        value = lat_ref[source].astype(F32)
        xs[0, pl.ds(source * per_source, per_source), :] = value
        xs[1, pl.ds(source * per_source, per_source), :] = pltpu.roll(value, 64, 1)
    window_zero, act_zero = block + 4, block + 2
    for windows in (windows_a, windows_b):
        windows[window_zero] = jnp.zeros(windows.shape[1:], BF16)
    for act in (act_a, act_b):
        act[act_zero] = jnp.zeros((F, COLS, channels), BF16)
    gain = gain_ref[...]

    def clip_edges(at):
        is_first = (at == edge) | (at == edge + height)
        is_last = (at == edge - 1) | (at == edge - 1 + height)
        return is_first, is_last

    def fill(row, windows, into):
        lane = lax.broadcasted_iota(jnp.int32, (8, LANES), 1)
        col = lax.broadcasted_iota(jnp.int32, (8, LANES), 0)
        low = (lane < 16) | (lane >= 96)
        left_end = (col == 0) & ((lane & 63) < 16)
        right_end = (col == 7) & ((lane & 63) >= 32) & ((lane & 63) < 48)
        stack_row = jnp.clip(start - 2 + row, 0, units * owners - 1)
        source = lax.rem(stack_row, owners)
        unit = first_unit(start, 2, source, owners, units, capacity)
        slot = jnp.clip(lax.div(stack_row, owners) - unit, 0, capacity - 1)
        base = source * per_source + slot * 12
        rolled = [{}, {}]
        for frame in range(CT + F):
            for half in range(2):
                at_row = pl.ds(base + half * (CT + F) + frame, 1)
                for turn in range(2):
                    if turn == 1 and not 1 <= frame <= F:
                        continue
                    value = jnp.broadcast_to(xs[turn, at_row, :], (8, LANES))
                    rolled[turn][half, frame] = pltpu.roll(value, 0, 1, stride=16, stride_axis=0)
        for frame in range(F):
            pair = [
                jnp.where(low, rolled[0][half, frame], rolled[1][half, frame + 1])
                for half in range(2)
            ]
            last = [rolled[0][half, frame + 2] for half in range(2)]
            for lanes, (left, right) in enumerate((pair, last)):
                near = jnp.where(left_end, 0.0, jnp.where(right_end, right, left))
                far = jnp.where(right_end, 0.0, jnp.where(left_end, left, right))
                windows[
                    into,
                    frame * COLS : (frame + 1) * COLS,
                    lanes * LANES : (lanes + 1) * LANES,
                ] = jnp.concatenate([near, far], axis=0).astype(BF16)

    def produce(row, count, into, windows, first, act):
        for at in range(count + 2):
            fill(row + at, windows, at)
        pieces = [[], [], []]
        for at in range(count):
            is_first, is_last = clip_edges(row + at)
            pieces[0].append(windows[jnp.where(is_first, window_zero, at)])
            pieces[1].append(windows[at + 1])
            pieces[2].append(windows[jnp.where(is_last, window_zero, at + 2)])
        slab = jnp.concatenate([jnp.concatenate(part, axis=0) for part in pieces], axis=1)
        sums = jnp.dot(slab, table[...], preferred_element_type=F32)
        first[into * size : (into + count) * size, :] = sums
        for at in range(count):
            value = sums[at * size : (at + 1) * size]
            mean_square = jnp.mean(value * value, axis=-1, keepdims=True)
            value = value * lax.rsqrt(mean_square + EPSILON) * gain
            value = value / (1.0 + jnp.exp(-value))
            act[into + at] = value.astype(BF16).reshape(F, COLS, channels)

    def copy_out(number):
        rows = pl.ds(number * block, block)
        return pltpu.make_async_copy(
            late.at[rows], out_ref.at[rows, pl.ds(2, 2)], out_sems.at[number]
        )

    def part_copy(number):
        rows = pl.ds(number * block, block)
        return pltpu.make_async_copy(part_ref.at[rows], part_out.at[rows], part_sems.at[number])

    early = pltpu.make_async_copy(weights.at[pl.ds(0, 6 * channels)], early_ref, early_sem)

    def convolve(number, first, act):
        begin = number * block
        source_rows = [[], [], []]
        for row in range(block):
            is_first, is_last = clip_edges(begin + row + 1)
            source_rows[0].append(jnp.where(is_first, act_zero, row))
            source_rows[1].append(row + 1)
            source_rows[2].append(jnp.where(is_last, act_zero, row + 2))

        def finish(frames, weight_from, frame_from, count):
            pieces = []
            for frame in frames:
                for row_tap in range(3):
                    parts = [
                        act[at, frame : frame + count].reshape(count * COLS, channels)
                        for at in source_rows[row_tap]
                    ]
                    pieces.append(jnp.concatenate(parts, axis=0))
            slab = jnp.concatenate(pieces, axis=1)
            sums = jnp.dot(slab, weights[weight_from:, :], preferred_element_type=F32)
            total = shift_columns(sums, channels)
            parts = []
            for row in range(block):
                at = (row + 1) * size + frame_from * COLS
                parts.append(first[at : at + count * COLS, :])
            return total + jnp.concatenate(parts, axis=0)

        taps = 3 * channels
        rows = pl.ds(begin, block)
        value = finish([0, 1, 2], 0, 2, 2)
        at_row = lax.broadcasted_iota(jnp.int32, value.shape, 0) // (2 * COLS)
        value = jnp.where(at_row < live - begin, value, 0.0)
        late[rows] = value.astype(BF16).reshape(block, 2, COLS, channels)
        part_ref[rows, 1] = finish([0, 1], taps, 1, 1).reshape(block, COLS, channels)
        part_ref[rows, 0] = finish([0], 2 * taps, 0, 1).reshape(block, COLS, channels)

    def step(number, first, act, next_windows, next_first, next_act):
        convolve(number, first, act)
        for row in range(2):
            next_act[row] = act[block + row]
        next_first[: 2 * size, :] = first[block * size :, :]
        produce((number + 1) * block + 2, block, 2, next_windows, next_first, next_act)
        copy_out(number).start()
        part_copy(number).start()

    produce(0, block + 2, 0, windows_a, first_a, act_a)
    for copy in copies:
        copy.wait()
    early.start()
    used = lax.div(live + block - 1, block)

    def two_steps(pair, carry):
        step(2 * pair, first_a, act_a, windows_b, first_b, act_b)

        @pl.when(2 * pair + 1 < used)
        def _():
            step(2 * pair + 1, first_b, act_b, windows_a, first_a, act_a)

        return carry

    lax.fori_loop(0, lax.div(used + 1, 2), two_steps, 0)

    def clear(number, carry):
        late[pl.ds(number * block, block)] = jnp.zeros((block, 2, COLS, channels), BF16)
        copy_out(number).start()
        return carry

    def finish_part(number, carry):
        part_copy(number).wait()
        return carry

    lax.fori_loop(used, blocks, clear, 0)
    lax.fori_loop(0, used, finish_part, 0)
    early.wait()
    for number in range(blocks):
        copy_out(number).wait()


def cached_frames(
    bands, cache, part_in, early_ref, late_ref, out_ref,
    weights, part_ref, early, out_sems, part_sems, early_sem,
    *, owners, units, capacity, height, block, band_max, channels,
):
    del late_ref
    group = lax.axis_index("seq")
    owner = lax.axis_index("dec")
    live = bands[group, owner]
    start = band_start(bands, group, owner, owners)
    depth = channels // LANES
    blocks = band_max // block
    edge = lax.rem(height - lax.rem(start - 1 + height, height), height)

    def slot_of(at):
        row = jnp.clip(start - 1 + at, 0, units * owners - 1)
        source = lax.rem(row, owners)
        unit = first_unit(start, 1, source, owners, units, capacity)
        return source * capacity + jnp.clip(lax.div(row, owners) - unit, 0, capacity - 1)

    def copy_out(number):
        rows = pl.ds(number * block, block)
        return pltpu.make_async_copy(
            early.at[rows], out_ref.at[rows, pl.ds(0, 2)], out_sems.at[number]
        )

    def part_copy(number):
        rows = pl.ds(number * block, block)
        return pltpu.make_async_copy(part_in.at[rows], part_ref.at[rows], part_sems.at[number])

    load = pltpu.make_async_copy(early_ref, weights, early_sem)
    load.start()
    used = lax.div(live + block - 1, block)

    def load_part(number, carry):
        part_copy(number).start()
        return carry

    part_copy(0).start()
    load.wait()
    lax.fori_loop(1, used, load_part, 0)

    def convolve(number, carry):
        part_copy(number).wait()
        begin = number * block
        edges, source_rows = [[], [], []], [[], [], []]
        for row in range(block):
            at = begin + row + 1
            edges[0].append((at == edge) | (at == edge + height))
            edges[1].append(None)
            edges[2].append((at == edge - 1) | (at == edge - 1 + height))
            for row_tap in range(3):
                source_rows[row_tap].append(slot_of(at + row_tap - 1))

        def slab(frames):
            pieces = []
            for frame in frames:
                for row_tap in range(3):
                    for part in range(depth):
                        from_tile = (frame * depth + part) * COLS
                        parts = []
                        for at, outside in zip(source_rows[row_tap], edges[row_tap]):
                            value = cache[at, from_tile : from_tile + COLS, :]
                            if outside is not None:
                                value = jnp.where(outside, jnp.zeros_like(value), value)
                            parts.append(value)
                        pieces.append(jnp.concatenate(parts, axis=0))
            return jnp.concatenate(pieces, axis=1)

        at_row = lax.broadcasted_iota(jnp.int32, (block * COLS, channels), 0) // COLS
        taps = 3 * channels
        rows = pl.ds(begin, block)
        for frame, frames in ((0, (0, 1)), (1, (1,))):
            sums = jnp.dot(
                slab(frames), weights[: len(frames) * taps, :], preferred_element_type=F32
            )
            total = shift_columns(sums, channels) + part_ref[rows, frame].reshape(
                block * COLS, channels
            )
            total = jnp.where(at_row < live - begin, total, 0.0)
            early[rows, frame] = total.astype(BF16).reshape(block, COLS, channels)
        copy_out(number).start()
        return carry

    lax.fori_loop(0, used, convolve, 0)

    def clear(number, carry):
        early[pl.ds(number * block, block)] = jnp.zeros((block, 2, COLS, channels), BF16)
        copy_out(number).start()
        return carry

    lax.fori_loop(used, blocks, clear, 0)
    for number in range(blocks):
        copy_out(number).wait()


def params(mebibytes, **extra):
    return pltpu.CompilerParams(vmem_limit_bytes=mebibytes * 1024 * 1024, **extra)


def shards(latents, cache_lat, cache_act, w_in, w_mid, norm_gain, clip_group, band_rows):
    groups = lax.axis_size("seq")
    owners = lax.axis_size("dec")
    clips = latents.shape[1]
    per_owner = latents.shape[2]
    channels = w_mid.shape[2]
    units = groups * per_owner
    height = per_owner * owners
    stack_rows = groups * height
    band_max = 2 * stack_rows // owners
    act_capacity = (band_max + 2 + owners - 1) // owners
    block = 8
    any_space = pl.BlockSpec(memory_space=pl.ANY)
    in_vmem = pl.BlockSpec(memory_space=pltpu.VMEM)
    in_hbm = pl.BlockSpec(memory_space=pltpu.HBM)

    def rows_first(array):
        return jnp.transpose(array[0, :, :, 0, :], (1, 0, 2))

    lat, old, act = rows_first(latents), rows_first(cache_lat), rows_first(cache_act)
    tiles = act.shape[2] // LANES
    lat_rows = (per_owner * 12 + 15) // 16 * 16
    per_step = 3
    cache_rows = per_owner * tiles
    packed = pl.pallas_call(
        functools.partial(
            pack_clips, per_owner=per_owner, per_step=per_step, clips=clips
        ),
        grid_spec=pltpu.PrefetchScalarGridSpec(
            num_scalar_prefetch=1,
            grid=(),
            in_specs=[in_hbm, in_hbm, in_hbm],
            out_specs=[in_vmem] * clips,
            scratch_shapes=[
                pltpu.VMEM(lat.shape, BF16),
                pltpu.VMEM(old.shape, BF16),
                pltpu.VMEM(act.shape, BF16),
                pltpu.VMEM((clips * lat_rows, LANES), F32),
                pltpu.VMEM((2, clips * per_step * tiles, LANES), F32),
                pltpu.SemaphoreType.DMA((2 + per_owner // per_step,)),
            ],
        ),
        out_shape=[jax.ShapeDtypeStruct((cache_rows + lat_rows, LANES), BF16)] * clips,
        compiler_params=params(48),
        name="pack_clips",
    )(clip_group, lat, old, act)

    def trade(parts):
        return [parts[0]] + [
            lax.ppermute(part, "seq", [(i, i ^ other) for i in range(groups)])
            for other, part in enumerate(parts)
            if other
        ]

    def exchange(array, axis):
        return lax.all_to_all(array, axis, split_axis=0, concat_axis=0, tiled=True)

    traded = trade(packed)
    lat_capacity = (band_max + 4 + owners - 1) // owners
    slice_rows = (lat_capacity * 12 + 15) // 16 * 16
    band_lat = pl.pallas_call(
        functools.partial(
            slice_latents, owners=owners, units=units, capacity=lat_capacity, per_owner=per_owner,
            cache_rows=cache_rows,
        ),
        grid_spec=pltpu.PrefetchScalarGridSpec(
            num_scalar_prefetch=1,
            grid=(),
            in_specs=[in_vmem] * clips,
            out_specs=in_vmem,
            scratch_shapes=[pltpu.VMEM((units * 12 + slice_rows, LANES), F32)],
        ),
        out_shape=jax.ShapeDtypeStruct((owners, slice_rows, LANES), BF16),
        compiler_params=params(24),
        name="slice_latents",
    )(band_rows, *traded)
    band_lat = exchange(band_lat, "dec")
    band_act = pl.pallas_call(
        functools.partial(
            slice_caches, owners=owners, units=units, capacity=act_capacity, tiles=tiles
        ),
        grid_spec=pltpu.PrefetchScalarGridSpec(
            num_scalar_prefetch=1,
            grid=(),
            in_specs=[any_space] * clips,
            out_specs=any_space,
            scratch_shapes=[
                pltpu.VMEM((units * tiles, LANES), BF16),
                pltpu.SemaphoreType.DMA((clips,)),
                pltpu.SemaphoreType.DMA((owners,)),
            ],
        ),
        out_shape=jax.ShapeDtypeStruct((owners, act_capacity * tiles, LANES), BF16),
        compiler_params=params(24),
        name="slice_caches",
    )(band_rows, *traded)
    band_lat, band_act = lax.optimization_barrier((band_lat, band_act))
    band_act = exchange(band_act, "dec")

    late, part, early_mid = pl.pallas_call(
        functools.partial(
            new_frames, owners=owners, units=units, capacity=lat_capacity, height=height,
            block=block, band_max=band_max, channels=channels,
        ),
        grid_spec=pltpu.PrefetchScalarGridSpec(
            num_scalar_prefetch=1,
            grid=(),
            in_specs=[in_vmem, in_vmem, in_vmem, in_hbm],
            out_specs=[in_hbm, in_hbm, in_hbm],
            scratch_shapes=[
                pltpu.VMEM((9 * channels, 3 * channels), BF16),
                pltpu.VMEM((6 * LANES, channels), BF16),
                pltpu.VMEM((2, owners * slice_rows, LANES), F32),
                pltpu.VMEM((block + 5, F * COLS, 2 * LANES), BF16),
                pltpu.VMEM((block + 5, F * COLS, 2 * LANES), BF16),
                pltpu.VMEM(((block + 2) * F * COLS, channels), F32),
                pltpu.VMEM(((block + 2) * F * COLS, channels), F32),
                pltpu.VMEM((block + 3, F, COLS, channels), BF16),
                pltpu.VMEM((block + 3, F, COLS, channels), BF16),
                pltpu.VMEM((band_max, 2, COLS, channels), BF16),
                pltpu.VMEM((band_max, 2, COLS, channels), F32),
                pltpu.SemaphoreType.DMA((27,)),
                pltpu.SemaphoreType.DMA((band_max // block,)),
                pltpu.SemaphoreType.DMA((band_max // block,)),
                pltpu.SemaphoreType.DMA,
            ],
        ),
        out_shape=[
            jax.ShapeDtypeStruct((band_max, F, COLS, channels), BF16),
            jax.ShapeDtypeStruct((band_max, 2, COLS, channels), F32),
            jax.ShapeDtypeStruct((6 * channels, 3 * channels), BF16),
        ],
        compiler_params=params(44),
        cost_estimate=pl.CostEstimate(
            flops=2 * band_max * 9 * COLS * 9 * channels * channels,
            bytes_accessed=16 * 1024 * 1024,
            transcendentals=0,
        ),
        name="new_frames",
    )(band_rows, band_lat, w_in, norm_gain.reshape(1, channels), w_mid)

    slots = owners * act_capacity
    decoded = pl.pallas_call(
        functools.partial(
            cached_frames, owners=owners, units=units, capacity=act_capacity, height=height,
            block=block, band_max=band_max, channels=channels,
        ),
        grid_spec=pltpu.PrefetchScalarGridSpec(
            num_scalar_prefetch=1,
            grid=(),
            in_specs=[in_vmem, in_hbm, in_hbm, in_hbm],
            out_specs=in_hbm,
            scratch_shapes=[
                pltpu.VMEM((6 * channels, 3 * channels), BF16),
                pltpu.VMEM((band_max, 2, COLS, channels), F32),
                pltpu.VMEM((band_max, 2, COLS, channels), BF16),
                pltpu.SemaphoreType.DMA((band_max // block,)),
                pltpu.SemaphoreType.DMA((band_max // block,)),
                pltpu.SemaphoreType.DMA,
            ],
        ),
        out_shape=jax.ShapeDtypeStruct((band_max, F, COLS, channels), BF16),
        input_output_aliases={4: 0},
        compiler_params=params(36),
        cost_estimate=pl.CostEstimate(
            flops=2 * band_max * 3 * COLS * 9 * channels * channels,
            bytes_accessed=16 * 1024 * 1024,
            transcendentals=0,
        ),
        name="cached_frames",
    )(band_rows, band_act.reshape(slots, tiles, LANES), part, early_mid, late)
    return decoded.reshape((1, 1) + decoded.shape)


def solution(mesh):
    placed = (
        P("seq", None, None, "dec", None),
        P("seq", None, None, "dec", None),
        P("seq", None, None, "dec", None),
        P(),
        P(),
        P(),
        P(),
        P(),
    )
    return jax.shard_map(
        shards,
        mesh=mesh,
        in_specs=placed,
        out_specs=P("seq", "dec", None, None, None, None),
        check_vma=False,
    )
```

profile of v0, /device:TPU:2, one launch (start us, length us, event | category | flops | bytes accessed | tf_op | source)
XLA Modules:
  0.0 136.3 jit_solution(15239661152438878711)
XLA Ops:
  0.0 1.3 copy-done
  1.3 0.9 copy-done.1
  2.2 0.8 copy-done.2
  3.0 0.7 copy-done.6
  3.6 2.7 %pack_clips.1 = (bf16[1296,128]{1,0:T(8,128)(2,1)S(1)}, bf16[1296,128]{1,0:T(8,128)(2,1)S(1)}, bf16[1296,128]{1,0:T(8,128)(2,1)S(1)}, bf16[1296,128]{1,0:T(8,128)(2,1)S(1)}) custom-call(s32[4,4]{1,0:T(4,128)S(1)} %copy-done.6, bf16[12,4,1024]{2,1,0:T(4,128)(2,1)S(1)} %bitcast.13, bf16[12,4,512]{2,1,0:T(4,128)(2,1)S(1)} %bitcast.14, ...), custom_call_target="tpu_custom_call" | custom-call | tf_op jit(solution)/shard_map/pack_clips/pallas_call | solution.py:469
  6.4 0.1 collective-permute-start
  6.5 2.0 %collective-permute-start.1 = (bf16[1296,128]{1,0:T(8,128)(2,1)S(1)}, bf16[1296,128]{1,0:T(8,128)(2,1)S(1)}, u32[]{:S(2)}, u32[]{:S(2)}) collective-permute-start(bf16[1296,128]{1,0:T(8,128)(2,1)S(1)} %get-tuple-element.16), channel_id=1, source_target_pairs={{0,16},{8,24},{16,0},{24,8},{1,17},{9,25},{17,1},{25,9},{2,18},{10... | collective-permute-start | bytes 995336 | tf_op jit(solution)/shard_map/ppermute | solution.py:494
  8.5 1.4 %collective-permute-start.2 = (bf16[1296,128]{1,0:T(8,128)(2,1)S(1)}, bf16[1296,128]{1,0:T(8,128)(2,1)S(1)}, u32[]{:S(2)}, u32[]{:S(2)}) collective-permute-start(bf16[1296,128]{1,0:T(8,128)(2,1)S(1)} %get-tuple-element.17), channel_id=1, source_target_pairs={{0,24},{8,16},{16,8},{24,0},{1,25},{9,17},{17,9},{25,1},{2,26},{10... | collective-permute-start | bytes 995336 | tf_op jit(solution)/shard_map/ppermute | solution.py:494
  10.0 7.2 %collective-permute-done.refs_1_ = bf16[1296,128]{1,0:T(8,128)(2,1)S(1)} collective-permute-done((bf16[1296,128]{1,0:T(8,128)(2,1)S(1)}, bf16[1296,128]{1,0:T(8,128)(2,1)S(1)}, u32[]{:S(2)}, u32[]{:S(2)}) %collective-permute-start) | collective-permute-done | bytes 331808 | tf_op jit(solution)/shard_map/ppermute | solution.py:494
  17.2 5.3 %collective-permute-done.1.refs_2_ = bf16[1296,128]{1,0:T(8,128)(2,1)S(1)} collective-permute-done((bf16[1296,128]{1,0:T(8,128)(2,1)S(1)}, bf16[1296,128]{1,0:T(8,128)(2,1)S(1)}, u32[]{:S(2)}, u32[]{:S(2)}) %collective-permute-start.1) | collective-permute-done | bytes 331808 | tf_op jit(solution)/shard_map/ppermute | solution.py:494
  22.4 1.6 %collective-permute-done.2.refs_3_ = bf16[1296,128]{1,0:T(8,128)(2,1)S(1)} collective-permute-done((bf16[1296,128]{1,0:T(8,128)(2,1)S(1)}, bf16[1296,128]{1,0:T(8,128)(2,1)S(1)}, u32[]{:S(2)}, u32[]{:S(2)}) %collective-permute-start.2) | collective-permute-done | bytes 331808 | tf_op jit(solution)/shard_map/ppermute | solution.py:494
  24.1 0.7 copy-done.3
  24.7 1.8 %slice_latents.1 = bf16[8,160,128]{2,1,0:T(8,128)(2,1)} custom-call(s32[4,8]{1,0:T(4,128)S(1)} %copy-done.3, bf16[1296,128]{1,0:T(8,128)(2,1)S(1)} %get-tuple-element.14.refs_0_, bf16[1296,128]{1,0:T(8,128)(2,1)S(1)} %collective-permute-done.refs_1_, bf16[1296,128]{1,0:T(8,128)(2,1)S(1)} %collective-permute-done.1.refs_2_, ...), custom_call_target="tpu_custom_call" | custom-call | tf_op jit(solution)/shard_map/slice_latents/pallas_call | solution.py:505
  26.6 5.0 %all-to-all-start = ((bf16[8,160,128]{2,1,0:T(8,128)(2,1)}), bf16[8,160,128]{2,1,0:T(8,128)(2,1)S(1)}, u32[]{:S(2)}, u32[]{:S(2)}) async-start(bf16[8,160,128]{2,1,0:T(8,128)(2,1)} %slice_latents.1), calls=%async_computation | async-start | bytes 655360 | tf_op jit(solution)/shard_map/all_to_all | solution.py:500
  31.6 0.7 copy-done.4
  32.2 2.4 %slice_caches.1 = bf16[8,1248,128]{2,1,0:T(8,128)(2,1)} custom-call(s32[4,8]{1,0:T(4,128)S(1)} %copy-done.4, bf16[1296,128]{1,0:T(8,128)(2,1)S(1)} %get-tuple-element.14.refs_0_, bf16[1296,128]{1,0:T(8,128)(2,1)S(1)} %collective-permute-done.refs_1_, bf16[1296,128]{1,0:T(8,128)(2,1)S(1)} %collective-permute-done.1.refs_2_, ...), custom_call_target="tpu_custom_call" | custom-call | tf_op jit(solution)/shard_map/slice_caches/pallas_call | solution.py:522
  34.7 8.0 %all-to-all-done.lat_ref = bf16[8,160,128]{2,1,0:T(8,128)(2,1)S(1)} async-done(((bf16[8,160,128]{2,1,0:T(8,128)(2,1)}), bf16[8,160,128]{2,1,0:T(8,128)(2,1)S(1)}, u32[]{:S(2)}, u32[]{:S(2)}) %all-to-all-start) | async-done | bytes 327712 | tf_op jit(solution)/shard_map/all_to_all | solution.py:500
  42.7 3.6 %all-to-all-start.1 = ((bf16[8,1248,128]{2,1,0:T(8,128)(2,1)}), bf16[8,1248,128]{2,1,0:T(8,128)(2,1)S(1)}, u32[]{:S(2)}, u32[]{:S(2)}) async-start(bf16[8,1248,128]{2,1,0:T(8,128)(2,1)} %slice_caches.1), calls=%async_computation.1 | async-start | bytes 5111808 | tf_op jit(solution)/shard_map/all_to_all | solution.py:500
  46.4 61.1 %new_frames.1 = (bf16[96,4,16,384]{3,2,1,0:T(8,128)(2,1)}, f32[96,2,16,384]{3,2,1,0:T(8,128)S(1)}, bf16[2304,1152]{1,0:T(8,128)(2,1)}) custom-call(s32[4,8]{1,0:T(4,128)S(1)} %copy-done.5, bf16[8,160,128]{2,1,0:T(8,128)(2,1)S(1)} %all-to-all-done.lat_ref, bf16[27,16,384]{2,1,0:T(8,128)(2,1)S(1)} %copy-done.7, f32[1,384]{1,0:T(1,128)S(1)} %reshape.10.gain_ref, ...), custom_call_target="tpu_custom_call" | custom-call | flops 36691771392 | bytes 16777216 | tf_op jit(solution)/shard_map/new_frames/pallas_call | solution.py:544
  107.5 2.2 %copy-done.9 = f32[96,2,16,384]{3,2,1,0:T(8,128)} copy-done((f32[96,2,16,384]{3,2,1,0:T(8,128)}, f32[96,2,16,384]{3,2,1,0:T(8,128)S(1)}, u32[]{:S(2)}) %copy-start.9) | copy-done | bytes 4718616
  109.6 0.0 all-to-all-done.1
  109.6 2.5 %copy-done.8 = bf16[2304,1152]{1,0:T(8,128)(2,1)S(1)} copy-done((bf16[2304,1152]{1,0:T(8,128)(2,1)S(1)}, bf16[2304,1152]{1,0:T(8,128)(2,1)}, u32[]{:S(2)}) %copy-start.8) | copy-done | bytes 5308440
  112.1 2.3 %copy-done.10 = f32[96,2,16,384]{3,2,1,0:T(8,128)S(1)} copy-done((f32[96,2,16,384]{3,2,1,0:T(8,128)S(1)}, f32[96,2,16,384]{3,2,1,0:T(8,128)}, u32[]{:S(2)}) %copy-start.10) | copy-done | bytes 4718616
  114.5 21.6 %cached_frames.1 = bf16[96,4,16,384]{3,2,1,0:T(8,128)(2,1)} custom-call(s32[4,8]{1,0:T(4,128)S(1)} %copy-done.5, bf16[104,96,128]{2,1,0:T(8,128)(2,1)S(1)} %bitcast.11, f32[96,2,16,384]{3,2,1,0:T(8,128)S(1)} %copy-done.10, bf16[2304,1152]{1,0:T(8,128)(2,1)S(1)} %copy-done.8, ...), custom_call_target="tpu_custom_call", output_to_operand_aliasing={{}: (4, {})} | custom-call | flops 12230590464 | bytes 16777216 | tf_op jit(solution)/shard_map/cached_frames/pallas_call | solution.py:587
  (16 shorter events, 0.0 us)
Async XLA Ops:
  0.0 1.3 copy-start
  1.3 0.9 copy-start.1
  2.2 0.8 copy-start.2
  3.0 0.7 copy-start.6
  6.4 10.8 %collective-permute-start = (bf16[1296,128]{1,0:T(8,128)(2,1)S(1)}, bf16[1296,128]{1,0:T(8,128)(2,1)S(1)}, u32[]{:S(2)}, u32[]{:S(2)}) collective-permute-start(bf16[1296,128]{1,0:T(8,128)(2,1)S(1)} %get-tuple-element.15), channel_id=1, source_target_pairs={{0,8},{8,0},{16,24},{24,16},{1,9},{9,1},{17,25},{25,17},{2,10},{10... | collective-permute-start | bytes 995336 | tf_op jit(solution)/shard_map/ppermute | solution.py:494
  6.5 16.0 %collective-permute-start.1 = (bf16[1296,128]{1,0:T(8,128)(2,1)S(1)}, bf16[1296,128]{1,0:T(8,128)(2,1)S(1)}, u32[]{:S(2)}, u32[]{:S(2)}) collective-permute-start(bf16[1296,128]{1,0:T(8,128)(2,1)S(1)} %get-tuple-element.16), channel_id=1, source_target_pairs={{0,16},{8,24},{16,0},{24,8},{1,17},{9,25},{17,1},{25,9},{2,18},{10... | collective-permute-start | bytes 995336 | tf_op jit(solution)/shard_map/ppermute | solution.py:494
  8.5 15.6 %collective-permute-start.2 = (bf16[1296,128]{1,0:T(8,128)(2,1)S(1)}, bf16[1296,128]{1,0:T(8,128)(2,1)S(1)}, u32[]{:S(2)}, u32[]{:S(2)}) collective-permute-start(bf16[1296,128]{1,0:T(8,128)(2,1)S(1)} %get-tuple-element.17), channel_id=1, source_target_pairs={{0,24},{8,16},{16,8},{24,0},{1,25},{9,17},{17,9},{25,1},{2,26},{10... | collective-permute-start | bytes 995336 | tf_op jit(solution)/shard_map/ppermute | solution.py:494
  24.1 0.7 copy-start.3
  26.6 19.8 %copy-start.11 = (f32[384]{0:T(512)S(1)}, f32[384]{0:T(512)}, u32[]{:S(2)}) copy-start(f32[384]{0:T(512)} %param.13) | copy-start | bytes 4612
  26.6 19.8 %copy-start.5 = (s32[4,8]{1,0:T(4,128)S(1)}, s32[4,8]{1,0:T(4,128)}, u32[]{:S(2)}) copy-start(s32[4,8]{1,0:T(4,128)} %bands.7) | copy-start | bytes 388
  26.6 19.8 %copy-start.7 = (bf16[27,16,384]{2,1,0:T(8,128)(2,1)S(1)}, bf16[27,16,384]{2,1,0:T(8,128)(2,1)}, u32[]{:S(2)}) copy-start(bf16[27,16,384]{2,1,0:T(8,128)(2,1)} %win_ref.1) | copy-start | bytes 995332
  26.6 16.2 %all-to-all-start = ((bf16[8,160,128]{2,1,0:T(8,128)(2,1)}), bf16[8,160,128]{2,1,0:T(8,128)(2,1)S(1)}, u32[]{:S(2)}, u32[]{:S(2)}) async-start(bf16[8,160,128]{2,1,0:T(8,128)(2,1)} %slice_latents.1), calls=%async_computation | async-start | bytes 655360 | tf_op jit(solution)/shard_map/all_to_all | solution.py:500
  31.6 0.7 copy-start.4
  42.7 66.9 %all-to-all-start.1 = ((bf16[8,1248,128]{2,1,0:T(8,128)(2,1)}), bf16[8,1248,128]{2,1,0:T(8,128)(2,1)S(1)}, u32[]{:S(2)}, u32[]{:S(2)}) async-start(bf16[8,1248,128]{2,1,0:T(8,128)(2,1)} %slice_caches.1), calls=%async_computation.1 | async-start | bytes 5111808 | tf_op jit(solution)/shard_map/all_to_all | solution.py:500
  107.5 2.2 %copy-start.9 = (f32[96,2,16,384]{3,2,1,0:T(8,128)}, f32[96,2,16,384]{3,2,1,0:T(8,128)S(1)}, u32[]{:S(2)}) copy-start(f32[96,2,16,384]{3,2,1,0:T(8,128)S(1)} %get-tuple-element.20.part_in) | copy-start | bytes 14155780
  109.6 2.5 %copy-start.8 = (bf16[2304,1152]{1,0:T(8,128)(2,1)S(1)}, bf16[2304,1152]{1,0:T(8,128)(2,1)}, u32[]{:S(2)}) copy-start(bf16[2304,1152]{1,0:T(8,128)(2,1)} %get-tuple-element.21.early_ref) | copy-start | bytes 15925252
  112.1 2.3 %copy-start.10 = (f32[96,2,16,384]{3,2,1,0:T(8,128)S(1)}, f32[96,2,16,384]{3,2,1,0:T(8,128)}, u32[]{:S(2)}) copy-start(f32[96,2,16,384]{3,2,1,0:T(8,128)} %copy-done.9) | copy-start | bytes 14155780
where the time goes:
time: 138 us; the launch traced here: 136 us
  Pallas kernels  89.7 us (65%)
  waiting for transfers between devices  22.2 us (16%)
  starting transfers between devices  12.2 us (9%)
  local copies, waits for them, and re-layouts  12 us (9%)
    pallas_call x1, Pallas kernels, shards(): pl.pallas_call(functools.partial(new_frames, owners=owners, units=units,...  61.1 us
    pallas_call x1, Pallas kernels, shards(): pl.pallas_call(functools.partial(cached_frames, owners=owners, units=unit...  21.6 us
    ppermute x3, waiting for transfers between devices, trade(): lax.ppermute(part, 'seq', [(i, i ^ other) for i in range(groups)])  14.1 us
    unnamed x24, local copies, waits for them, and re-layouts  12 us
    all_to_all x2, starting transfers between devices, exchange(): return lax.all_to_all(array, axis, split_axis=0, concat_axis=0, tiled=True)  8.63 us
    all_to_all x2, waiting for transfers between devices, exchange(): return lax.all_to_all(array, axis, split_axis=0, concat_axis=0, tiled=True)  8.05 us
    ppermute x3, starting transfers between devices, trade(): lax.ppermute(part, 'seq', [(i, i ^ other) for i in range(groups)])  3.55 us
  transfers between devices with their start and end apart: 5, of which 4 were waited for; matrix products, arithmetic and copies ran while one was open for 0% of the time, Pallas kernels for 47%

commit v1 on v0

--- a/solution.py
+++ b/solution.py
@@ -36,7 +36,8 @@
 
 
 def pack_clips(groups_ref, lat_in, old_in, act_in, *refs, per_owner, per_step, clips):
-    *outs, lat_ref, old_ref, act_ref, lat_scratch, act_scratch, sems = refs
+    lat_outs, act_outs = refs[:clips], refs[clips : 2 * clips]
+    lat_ref, old_ref, act_ref, lat_scratch, act_scratch, sems = refs[2 * clips :]
     shard = lax.axis_index("seq")
     copies = [
         pltpu.make_async_copy(lat_in, lat_ref, sems.at[0]),
@@ -54,7 +55,7 @@
     tiles = act_ref.shape[2] // LANES
     depth = tiles // (CT * COLS)
     size = per_step * tiles
-    lat_rows = outs[0].shape[0] - per_owner * tiles
+    lat_rows = lat_outs[0].shape[0]
     copies[0].wait()
     copies[1].wait()
     for row in range(per_owner):
@@ -68,9 +69,9 @@
                     value = lat_ref[row, :, tile * LANES : (tile + 1) * LANES]
                 at = row * 12 + half * (CT + F) + frame
                 lat_scratch[pl.ds(at, clips, stride=lat_rows), :] = value.astype(F32)
-    for out, clip in zip(outs, chosen):
+    for out, clip in zip(lat_outs, chosen):
         rows = pl.ds(pl.multiple_of(clip * lat_rows, 8), lat_rows)
-        out[per_owner * tiles :, :] = lat_scratch[rows, :].astype(BF16)
+        out[...] = lat_scratch[rows, :].astype(BF16)
     for step in range(steps):
         copies[2 + step].wait()
         for row in range(per_step):
@@ -83,19 +84,19 @@
                             step * per_step + row, :, tile * LANES : (tile + 1) * LANES
                         ]
                         act_scratch[step % 2, pl.ds(at, clips, stride=size), :] = value.astype(F32)
-        for out, clip in zip(outs, chosen):
+        for out, clip in zip(act_outs, chosen):
             rows = pl.ds(pl.multiple_of(clip * size, 8), size)
             out[step * size : (step + 1) * size, :] = act_scratch[step % 2, rows, :].astype(BF16)
 
 
-def slice_latents(bands, *refs, owners, units, capacity, per_owner, cache_rows):
+def slice_latents(bands, *refs, owners, units, capacity, per_owner):
     *ins, out_ref, scratch = refs
     group = lax.axis_index("seq")
     source = lax.axis_index("dec")
     rows = out_ref.shape[1]
     size = per_owner * 12
     for other, in_ref in enumerate(ins):
-        value = in_ref[cache_rows : cache_rows + size, :].astype(F32)
+        value = in_ref[:size, :].astype(F32)
         scratch[pl.ds((group ^ other) * size, size), :] = value
     value = pltpu.roll(scratch[: units * 12, :], 64, 1)
     lane = lax.broadcasted_iota(jnp.int32, value.shape, 1)
@@ -148,20 +149,16 @@
     return total + jnp.where(col < COLS - 1, right, 0.0)
 
 
-def weight_copies(mid_ref, weights, sems, channels):
-    copies = []
-    for tap in range(27):
-        into = weights.at[
-            pl.ds(tap // 3 * channels, channels), pl.ds(tap % 3 * channels, channels)
-        ]
-        copies.append(pltpu.make_async_copy(mid_ref.at[tap], into, sems.at[tap]))
-    return copies
+def widen_weights(mid_ref, _, out_ref):
+    channels = mid_ref.shape[1]
+    for tap in range(3):
+        out_ref[:, tap * channels : (tap + 1) * channels] = mid_ref[tap]
 
 
 def new_frames(
-    bands, lat_ref, win_ref, gain_ref, mid_ref, out_ref, part_out, early_ref, weights,
-    table, xs, windows_a, windows_b, first_a, first_b, act_a, act_b, late, part_ref,
-    sems, out_sems, part_sems, early_sem,
+    bands, lat_ref, win_ref, gain_ref, mid_ref, out_ref, part_out,
+    weights, table, xs, windows_a, windows_b, first_a, first_b, act_a, act_b, late, part_ref,
+    sem, out_sems, part_sems,
     *, owners, units, capacity, height, block, band_max, channels,
 ):
     group = lax.axis_index("seq")
@@ -172,9 +169,8 @@
     blocks = band_max // block
     size = F * COLS
     per_source = lat_ref.shape[1]
-    copies = weight_copies(mid_ref, weights, sems, channels)
-    for copy in copies:
-        copy.start()
+    load = pltpu.make_async_copy(mid_ref, weights, sem)
+    load.start()
     table[...] = jnp.zeros(table.shape, BF16)
     for time_tap in range(3):
         for row_tap in range(3):
@@ -233,9 +229,11 @@
                     lanes * LANES : (lanes + 1) * LANES,
                 ] = jnp.concatenate([near, far], axis=0).astype(BF16)
 
-    def produce(row, count, into, windows, first, act):
+    def fill_block(row, count, windows):
         for at in range(count + 2):
             fill(row + at, windows, at)
+
+    def convolve_first(row, count, windows):
         pieces = [[], [], []]
         for at in range(count):
             is_first, is_last = clip_edges(row + at)
@@ -243,7 +241,9 @@
             pieces[1].append(windows[at + 1])
             pieces[2].append(windows[jnp.where(is_last, window_zero, at + 2)])
         slab = jnp.concatenate([jnp.concatenate(part, axis=0) for part in pieces], axis=1)
-        sums = jnp.dot(slab, table[...], preferred_element_type=F32)
+        return jnp.dot(slab, table[...], preferred_element_type=F32)
+
+    def activate(sums, count, into, first, act):
         first[into * size : (into + count) * size, :] = sums
         for at in range(count):
             value = sums[at * size : (at + 1) * size]
@@ -261,8 +261,6 @@
     def part_copy(number):
         rows = pl.ds(number * block, block)
         return pltpu.make_async_copy(part_ref.at[rows], part_out.at[rows], part_sems.at[number])
-
-    early = pltpu.make_async_copy(weights.at[pl.ds(0, 6 * channels)], early_ref, early_sem)
 
     def convolve(number, first, act):
         begin = number * block
@@ -300,27 +298,29 @@
         part_ref[rows, 1] = finish([0, 1], taps, 1, 1).reshape(block, COLS, channels)
         part_ref[rows, 0] = finish([0], 2 * taps, 0, 1).reshape(block, COLS, channels)
 
-    def step(number, first, act, next_windows, next_first, next_act):
-        convolve(number, first, act)
+    def step(number, windows, first, act, next_windows, next_first, next_act):
+        sums = convolve_first((number + 1) * block + 2, block, windows)
         for row in range(2):
             next_act[row] = act[block + row]
         next_first[: 2 * size, :] = first[block * size :, :]
-        produce((number + 1) * block + 2, block, 2, next_windows, next_first, next_act)
+        activate(sums, block, 2, next_first, next_act)
+        convolve(number, first, act)
+        fill_block((number + 2) * block + 2, block, next_windows)
         copy_out(number).start()
         part_copy(number).start()
 
-    produce(0, block + 2, 0, windows_a, first_a, act_a)
-    for copy in copies:
-        copy.wait()
-    early.start()
+    fill_block(0, block + 2, windows_b)
+    activate(convolve_first(0, block + 2, windows_b), block + 2, 0, first_a, act_a)
+    fill_block(block + 2, block, windows_a)
+    load.wait()
     used = lax.div(live + block - 1, block)
 
     def two_steps(pair, carry):
-        step(2 * pair, first_a, act_a, windows_b, first_b, act_b)
+        step(2 * pair, windows_a, first_a, act_a, windows_b, first_b, act_b)
 
         @pl.when(2 * pair + 1 < used)
         def _():
-            step(2 * pair + 1, first_b, act_b, windows_a, first_a, act_a)
+            step(2 * pair + 1, windows_b, first_b, act_b, windows_a, first_a, act_a)
 
         return carry
 
@@ -337,7 +337,6 @@
 
     lax.fori_loop(used, blocks, clear, 0)
     lax.fori_loop(0, used, finish_part, 0)
-    early.wait()
     for number in range(blocks):
         copy_out(number).wait()
 
@@ -372,7 +371,7 @@
         rows = pl.ds(number * block, block)
         return pltpu.make_async_copy(part_in.at[rows], part_ref.at[rows], part_sems.at[number])
 
-    load = pltpu.make_async_copy(early_ref, weights, early_sem)
+    load = pltpu.make_async_copy(early_ref.at[pl.ds(0, 6 * channels)], weights, early_sem)
     load.start()
     used = lax.div(live + block - 1, block)
 
@@ -453,7 +452,8 @@
     stack_rows = groups * height
     band_max = 2 * stack_rows // owners
     act_capacity = (band_max + 2 + owners - 1) // owners
-    block = 8
+    block = next(size for size in (16, 8) if band_max % size == 0)
+    cached_block = next(size for size in (32, 16, 8) if band_max % size == 0)
     any_space = pl.BlockSpec(memory_space=pl.ANY)
     in_vmem = pl.BlockSpec(memory_space=pltpu.VMEM)
     in_hbm = pl.BlockSpec(memory_space=pltpu.HBM)
@@ -465,7 +465,6 @@
     tiles = act.shape[2] // LANES
     lat_rows = (per_owner * 12 + 15) // 16 * 16
     per_step = 3
-    cache_rows = per_owner * tiles
     packed = pl.pallas_call(
         functools.partial(
             pack_clips, per_owner=per_owner, per_step=per_step, clips=clips
@@ -474,7 +473,7 @@
             num_scalar_prefetch=1,
             grid=(),
             in_specs=[in_hbm, in_hbm, in_hbm],
-            out_specs=[in_vmem] * clips,
+            out_specs=[in_vmem] * (2 * clips),
             scratch_shapes=[
                 pltpu.VMEM(lat.shape, BF16),
                 pltpu.VMEM(old.shape, BF16),
@@ -484,10 +483,28 @@
                 pltpu.SemaphoreType.DMA((2 + per_owner // per_step,)),
             ],
         ),
-        out_shape=[jax.ShapeDtypeStruct((cache_rows + lat_rows, LANES), BF16)] * clips,
-        compiler_params=params(48),
+        out_shape=[jax.ShapeDtypeStruct((lat_rows, LANES), BF16)] * clips
+        + [jax.ShapeDtypeStruct((per_owner * tiles, LANES), BF16)] * clips,
+        compiler_params=params(56),
         name="pack_clips",
     )(clip_group, lat, old, act)
+
+    after_pack = packed[0]
+    wide_mid = pl.pallas_call(
+        widen_weights,
+        grid=(9,),
+        in_specs=[
+            pl.BlockSpec((3, channels, channels), lambda step: (step, 0, 0)),
+            any_space,
+        ],
+        out_specs=pl.BlockSpec((channels, 3 * channels), lambda step: (step, 0)),
+        out_shape=jax.ShapeDtypeStruct((9 * channels, 3 * channels), BF16),
+        compiler_params=params(40, dimension_semantics=("arbitrary",)),
+        cost_estimate=pl.CostEstimate(
+            flops=0, bytes_accessed=4 * 27 * channels * channels, transcendentals=0
+        ),
+        name="widen_weights",
+    )(w_mid, after_pack)
 
     def trade(parts):
         return [parts[0]] + [
@@ -499,13 +516,11 @@
     def exchange(array, axis):
         return lax.all_to_all(array, axis, split_axis=0, concat_axis=0, tiled=True)
 
-    traded = trade(packed)
     lat_capacity = (band_max + 4 + owners - 1) // owners
     slice_rows = (lat_capacity * 12 + 15) // 16 * 16
     band_lat = pl.pallas_call(
         functools.partial(
             slice_latents, owners=owners, units=units, capacity=lat_capacity, per_owner=per_owner,
-            cache_rows=cache_rows,
         ),
         grid_spec=pltpu.PrefetchScalarGridSpec(
             num_scalar_prefetch=1,
@@ -517,7 +532,7 @@
         out_shape=jax.ShapeDtypeStruct((owners, slice_rows, LANES), BF16),
         compiler_params=params(24),
         name="slice_latents",
-    )(band_rows, *traded)
+    )(band_rows, *trade(packed[:clips]))
     band_lat = exchange(band_lat, "dec")
     band_act = pl.pallas_call(
         functools.partial(
@@ -537,11 +552,11 @@
         out_shape=jax.ShapeDtypeStruct((owners, act_capacity * tiles, LANES), BF16),
         compiler_params=params(24),
         name="slice_caches",
-    )(band_rows, *traded)
+    )(band_rows, *trade(packed[clips:]))
     band_lat, band_act = lax.optimization_barrier((band_lat, band_act))
     band_act = exchange(band_act, "dec")
 
-    late, part, early_mid = pl.pallas_call(
+    late, part = pl.pallas_call(
         functools.partial(
             new_frames, owners=owners, units=units, capacity=lat_capacity, height=height,
             block=block, band_max=band_max, channels=channels,
@@ -550,7 +565,7 @@
             num_scalar_prefetch=1,
             grid=(),
             in_specs=[in_vmem, in_vmem, in_vmem, in_hbm],
-            out_specs=[in_hbm, in_hbm, in_hbm],
+            out_specs=[in_hbm, in_hbm],
             scratch_shapes=[
                 pltpu.VMEM((9 * channels, 3 * channels), BF16),
                 pltpu.VMEM((6 * LANES, channels), BF16),
@@ -563,16 +578,14 @@
                 pltpu.VMEM((block + 3, F, COLS, channels), BF16),
                 pltpu.VMEM((band_max, 2, COLS, channels), BF16),
                 pltpu.VMEM((band_max, 2, COLS, channels), F32),
-                pltpu.SemaphoreType.DMA((27,)),
+                pltpu.SemaphoreType.DMA,
                 pltpu.SemaphoreType.DMA((band_max // block,)),
                 pltpu.SemaphoreType.DMA((band_max // block,)),
-                pltpu.SemaphoreType.DMA,
             ],
         ),
         out_shape=[
             jax.ShapeDtypeStruct((band_max, F, COLS, channels), BF16),
             jax.ShapeDtypeStruct((band_max, 2, COLS, channels), F32),
-            jax.ShapeDtypeStruct((6 * channels, 3 * channels), BF16),
         ],
         compiler_params=params(44),
         cost_estimate=pl.CostEstimate(
@@ -581,13 +594,13 @@
             transcendentals=0,
         ),
         name="new_frames",
-    )(band_rows, band_lat, w_in, norm_gain.reshape(1, channels), w_mid)
+    )(band_rows, band_lat, w_in, norm_gain.reshape(1, channels), wide_mid)
 
     slots = owners * act_capacity
     decoded = pl.pallas_call(
         functools.partial(
             cached_frames, owners=owners, units=units, capacity=act_capacity, height=height,
-            block=block, band_max=band_max, channels=channels,
+            block=cached_block, band_max=band_max, channels=channels,
         ),
         grid_spec=pltpu.PrefetchScalarGridSpec(
             num_scalar_prefetch=1,
@@ -598,21 +611,21 @@
                 pltpu.VMEM((6 * channels, 3 * channels), BF16),
                 pltpu.VMEM((band_max, 2, COLS, channels), F32),
                 pltpu.VMEM((band_max, 2, COLS, channels), BF16),
-                pltpu.SemaphoreType.DMA((band_max // block,)),
-                pltpu.SemaphoreType.DMA((band_max // block,)),
+                pltpu.SemaphoreType.DMA((band_max // cached_block,)),
+                pltpu.SemaphoreType.DMA((band_max // cached_block,)),
                 pltpu.SemaphoreType.DMA,
             ],
         ),
         out_shape=jax.ShapeDtypeStruct((band_max, F, COLS, channels), BF16),
         input_output_aliases={4: 0},
-        compiler_params=params(36),
+        compiler_params=params(56),
         cost_estimate=pl.CostEstimate(
             flops=2 * band_max * 3 * COLS * 9 * channels * channels,
             bytes_accessed=16 * 1024 * 1024,
             transcendentals=0,
         ),
         name="cached_frames",
-    )(band_rows, band_act.reshape(slots, tiles, LANES), part, early_mid, late)
+    )(band_rows, band_act.reshape(slots, tiles, LANES), part, wide_mid, late)
     return decoded.reshape((1, 1) + decoded.shape)
 
 

time: 138 us -> 140 us (1.014)
  the two profiles are of different devices: /device:TPU:2 before, /device:TPU:12 now
where the time goes in v1:
time: 140 us; the launch traced here: 139 us
  Pallas kernels  94.4 us (67%)
  starting transfers between devices  17.6 us (13%)
  waiting for transfers between devices  16.6 us (12%)
  local copies, waits for them, and re-layouts  9.8 us (7%)
    pallas_call x1, Pallas kernels, shards(): pl.pallas_call(functools.partial(new_frames, owners=owners, units=units,...  57.3 us
    pallas_call x1, Pallas kernels, shards(): pl.pallas_call(functools.partial(cached_frames, owners=owners, units=unit...  21.9 us
    ppermute x6, waiting for transfers between devices, trade(): lax.ppermute(part, 'seq', [(i, i ^ other) for i in range(groups)])  16.6 us
    all_to_all x2, starting transfers between devices, exchange(): return lax.all_to_all(array, axis, split_axis=0, concat_axis=0, tiled=True)  10.6 us
    unnamed x22, local copies, waits for them, and re-layouts  9.8 us
    ppermute x6, starting transfers between devices, trade(): lax.ppermute(part, 'seq', [(i, i ^ other) for i in range(groups)])  7.04 us
    pallas_call x1, Pallas kernels, shards(): pl.pallas_call(widen_weights, grid=(9,), in_specs=[pl.BlockSpec((3, chann...  6.52 us
    pallas_call x1, Pallas kernels, shards(): pl.pallas_call(functools.partial(pack_clips, per_owner=per_owner, per_ste...  4.34 us
  transfers between devices with their start and end apart: 8, of which 6 were waited for; matrix products, arithmetic and copies ran while one was open for 0% of the time, Pallas kernels for 48%

profile of v1, /device:TPU:12, one launch (start us, length us, event | category | flops | bytes accessed | tf_op | source)
XLA Modules:
  0.0 138.7 jit_solution(4944573267742987249)
XLA Ops:
  0.0 4.3 %pack_clips.1 = (bf16[144,128]{1,0:T(8,128)(2,1)}, bf16[144,128]{1,0:T(8,128)(2,1)}, bf16[144,128]{1,0:T(8,128)(2,1)}, bf16[144,128]{1,0:T(8,128)(2,1)}, bf16[11...) custom-call(s32[4,4]{1,0:T(4,128)} %groups_ref.1, ...), custom_call_target="tpu_custom_call" | custom-call | tf_op jit(solution)/shard_map/pack_clips/pallas_call | solution.py:468
  4.4 1.6 %collective-permute-start = (bf16[144,128]{1,0:T(8,128)(2,1)}, bf16[144,128]{1,0:T(8,128)(2,1)S(1)}, u32[]{:S(2)}, u32[]{:S(2)}) collective-permute-start(bf16[144,128]{1,0:T(8,128)(2,1)} %get-tuple-element.18), channel_id=1, source_target_pairs={{0,8},{8,0},{16,24},{24,16},{1,9},{9,1},{17,25},{25,17},{2,10},{10... | collective-permute-start | bytes 110600 | tf_op jit(solution)/shard_map/ppermute | solution.py:511
  6.4 1.5 %collective-permute-start.2 = (bf16[144,128]{1,0:T(8,128)(2,1)}, bf16[144,128]{1,0:T(8,128)(2,1)S(1)}, u32[]{:S(2)}, u32[]{:S(2)}) collective-permute-start(bf16[144,128]{1,0:T(8,128)(2,1)} %get-tuple-element.20), channel_id=1, source_target_pairs={{0,24},{8,16},{16,8},{24,0},{1,25},{9,17},{17,9},{25,1},{2,26},{10... | collective-permute-start | bytes 110600 | tf_op jit(solution)/shard_map/ppermute | solution.py:511
  7.9 0.7 collective-permute-done.refs_1_
  8.6 1.6 %collective-permute-done.1.refs_2_ = bf16[144,128]{1,0:T(8,128)(2,1)S(1)} collective-permute-done((bf16[144,128]{1,0:T(8,128)(2,1)}, bf16[144,128]{1,0:T(8,128)(2,1)S(1)}, u32[]{:S(2)}, u32[]{:S(2)}) %collective-permute-start.1) | collective-permute-done | bytes 36896 | tf_op jit(solution)/shard_map/ppermute | solution.py:511
  10.2 1.3 collective-permute-done.2.refs_3_
  11.5 0.8 copy-done.2
  12.3 0.7 copy-done.4
  12.9 1.8 %slice_latents.1 = bf16[8,160,128]{2,1,0:T(8,128)(2,1)} custom-call(s32[4,8]{1,0:T(4,128)S(1)} %copy-done.4, bf16[144,128]{1,0:T(8,128)(2,1)S(1)} %copy-done.2, bf16[144,128]{1,0:T(8,128)(2,1)S(1)} %collective-permute-done.refs_1_, bf16[144,128]{1,0:T(8,128)(2,1)S(1)} %collective-permute-done.1.refs_2_, bf16[144,128]{1,0:T(8,128)(2,1)S(1)} %collective-permute-done.2.refs_3_), custom_call_target="tpu_custom_call" | custom-call | tf_op jit(solution)/shard_map/slice_latents/pallas_call | solution.py:521
  14.7 5.5 %all-to-all-start = ((bf16[8,160,128]{2,1,0:T(8,128)(2,1)}), bf16[8,160,128]{2,1,0:T(8,128)(2,1)S(1)}, u32[]{:S(2)}, u32[]{:S(2)}) async-start(bf16[8,160,128]{2,1,0:T(8,128)(2,1)} %slice_latents.1), calls=%async_computation | async-start | bytes 655360 | tf_op jit(solution)/shard_map/all_to_all | solution.py:517
  20.7 1.5 %collective-permute-start.4 = (bf16[1152,128]{1,0:T(8,128)(2,1)}, bf16[1152,128]{1,0:T(8,128)(2,1)S(1)}, u32[]{:S(2)}, u32[]{:S(2)}) collective-permute-start(bf16[1152,128]{1,0:T(8,128)(2,1)} %get-tuple-element.23), channel_id=1, source_target_pairs={{0,16},{8,24},{16,0},{24,8},{1,17},{9,25},{17,1},{25,9},{2,18},{10... | collective-permute-start | bytes 884744 | tf_op jit(solution)/shard_map/ppermute | solution.py:511
  22.3 1.4 %collective-permute-start.5 = (bf16[1152,128]{1,0:T(8,128)(2,1)}, bf16[1152,128]{1,0:T(8,128)(2,1)S(1)}, u32[]{:S(2)}, u32[]{:S(2)}) collective-permute-start(bf16[1152,128]{1,0:T(8,128)(2,1)} %get-tuple-element.24), channel_id=1, source_target_pairs={{0,24},{8,16},{16,8},{24,0},{1,25},{9,17},{17,9},{25,1},{2,26},{10... | collective-permute-start | bytes 884744 | tf_op jit(solution)/shard_map/ppermute | solution.py:511
  23.7 6.6 %collective-permute-done.3.refs_1_ = bf16[1152,128]{1,0:T(8,128)(2,1)S(1)} collective-permute-done((bf16[1152,128]{1,0:T(8,128)(2,1)}, bf16[1152,128]{1,0:T(8,128)(2,1)S(1)}, u32[]{:S(2)}, u32[]{:S(2)}) %collective-permute-start.3) | collective-permute-done | bytes 294944 | tf_op jit(solution)/shard_map/ppermute | solution.py:511
  30.3 5.0 %collective-permute-done.4.refs_2_ = bf16[1152,128]{1,0:T(8,128)(2,1)S(1)} collective-permute-done((bf16[1152,128]{1,0:T(8,128)(2,1)}, bf16[1152,128]{1,0:T(8,128)(2,1)S(1)}, u32[]{:S(2)}, u32[]{:S(2)}) %collective-permute-start.4) | collective-permute-done | bytes 294944 | tf_op jit(solution)/shard_map/ppermute | solution.py:511
  35.2 1.5 %collective-permute-done.5.refs_3_ = bf16[1152,128]{1,0:T(8,128)(2,1)S(1)} collective-permute-done((bf16[1152,128]{1,0:T(8,128)(2,1)}, bf16[1152,128]{1,0:T(8,128)(2,1)S(1)}, u32[]{:S(2)}, u32[]{:S(2)}) %collective-permute-start.5) | collective-permute-done | bytes 294944 | tf_op jit(solution)/shard_map/ppermute | solution.py:511
  36.7 1.0 copy-done.1
  38.4 2.4 %slice_caches.1 = bf16[8,1248,128]{2,1,0:T(8,128)(2,1)} custom-call(s32[4,8]{1,0:T(4,128)S(1)} %copy-done.5, bf16[1152,128]{1,0:T(8,128)(2,1)S(1)} %copy-done.1, bf16[1152,128]{1,0:T(8,128)(2,1)S(1)} %collective-permute-done.3.refs_1_, bf16[1152,128]{1,0:T(8,128)(2,1)S(1)} %collective-permute-done.4.refs_2_, bf16[1152,128]{1,0:T(8,128)(2,1)S(1)} %collective-permute-done.5.refs_3_), custom_call_target="tpu_custom_call" | custom-call | tf_op jit(solution)/shard_map/slice_caches/pallas_call | solution.py:537
  40.8 5.1 %all-to-all-start.1 = ((bf16[8,1248,128]{2,1,0:T(8,128)(2,1)}), bf16[8,1248,128]{2,1,0:T(8,128)(2,1)S(1)}, u32[]{:S(2)}, u32[]{:S(2)}) async-start(bf16[8,1248,128]{2,1,0:T(8,128)(2,1)} %slice_caches.1), calls=%async_computation.1 | async-start | bytes 5111808 | tf_op jit(solution)/shard_map/all_to_all | solution.py:517
  46.0 6.5 %widen_weights.1.mid_ref.early_ref = bf16[3456,1152]{1,0:T(8,128)(2,1)S(1)} custom-call(bf16[27,384,384]{2,1,0:T(8,128)(2,1)} %mid_ref.1, bf16[144,128]{1,0:T(8,128)(2,1)S(1)} %copy-done.3), custom_call_target="tpu_custom_call" | custom-call | bytes 15925248 | tf_op jit(solution)/shard_map/widen_weights/pallas_call | solution.py:493
  52.5 3.1 %copy-done = bf16[3456,1152]{1,0:T(8,128)(2,1)} copy-done((bf16[3456,1152]{1,0:T(8,128)(2,1)}, bf16[3456,1152]{1,0:T(8,128)(2,1)S(1)}, u32[]{:S(2)}) %copy-start) | copy-done | bytes 7962648
  55.6 57.3 %new_frames.1 = (bf16[96,4,16,384]{3,2,1,0:T(8,128)(2,1)}, f32[96,2,16,384]{3,2,1,0:T(8,128)S(1)}) custom-call(s32[4,8]{1,0:T(4,128)S(1)} %copy-done.6, bf16[8,160,128]{2,1,0:T(8,128)(2,1)S(1)} %all-to-all-done.lat_ref, bf16[27,16,384]{2,1,0:T(8,128)(2,1)S(1)} %copy-done.7, f32[1,384]{1,0:T(1,128)S(1)} %reshape.10.gain_ref, bf16[3456,1152]{1,0:T(8,128)(2,1)} %copy-done), custom_call_target="tpu_custom_call" | custom-call | flops 36691771392 | bytes 16777216 | tf_op jit(solution)/shard_map/new_frames/pallas_call | solution.py:559
  112.9 2.1 %copy-done.8 = f32[96,2,16,384]{3,2,1,0:T(8,128)} copy-done((f32[96,2,16,384]{3,2,1,0:T(8,128)}, f32[96,2,16,384]{3,2,1,0:T(8,128)S(1)}, u32[]{:S(2)}) %copy-start.8) | copy-done | bytes 4718616
  115.1 1.5 %copy-done.9 = bf16[8,1248,128]{2,1,0:T(8,128)(2,1)} copy-done((bf16[8,1248,128]{2,1,0:T(8,128)(2,1)}, bf16[8,1248,128]{2,1,0:T(8,128)(2,1)S(1)}, u32[]{:S(2)}) %copy-start.9) | copy-done | bytes 2555928
  116.6 21.9 %cached_frames.1 = bf16[96,4,16,384]{3,2,1,0:T(8,128)(2,1)} custom-call(s32[4,8]{1,0:T(4,128)} %bands.7, bf16[104,96,128]{2,1,0:T(8,128)(2,1)} %bitcast.11, f32[96,2,16,384]{3,2,1,0:T(8,128)} %copy-done.8, bf16[3456,1152]{1,0:T(8,128)(2,1)} %copy-done, bf16[96,4,16,384]{3,2,1,0:T(8,128)(2,1)} %get-tuple-element.28.late_ref), custom_call_target="tpu_custom_call", output_to_operand_aliasing={{}: (4, {})} | custom-call | flops 12230590464 | bytes 16777216 | tf_op jit(solution)/shard_map/cached_frames/pallas_call | solution.py:600
  (21 shorter events, 1.8 us)
Async XLA Ops:
  4.4 4.2 %collective-permute-start = (bf16[144,128]{1,0:T(8,128)(2,1)}, bf16[144,128]{1,0:T(8,128)(2,1)S(1)}, u32[]{:S(2)}, u32[]{:S(2)}) collective-permute-start(bf16[144,128]{1,0:T(8,128)(2,1)} %get-tuple-element.18), channel_id=1, source_target_pairs={{0,8},{8,0},{16,24},{24,16},{1,9},{9,1},{17,25},{25,17},{2,10},{10... | collective-permute-start | bytes 110600 | tf_op jit(solution)/shard_map/ppermute | solution.py:511
  5.9 4.3 %collective-permute-start.1 = (bf16[144,128]{1,0:T(8,128)(2,1)}, bf16[144,128]{1,0:T(8,128)(2,1)S(1)}, u32[]{:S(2)}, u32[]{:S(2)}) collective-permute-start(bf16[144,128]{1,0:T(8,128)(2,1)} %get-tuple-element.19), channel_id=1, source_target_pairs={{0,16},{8,24},{16,0},{24,8},{1,17},{9,25},{17,1},{25,9},{2,18},{10... | collective-permute-start | bytes 110600 | tf_op jit(solution)/shard_map/ppermute | solution.py:511
  6.4 5.1 %collective-permute-start.2 = (bf16[144,128]{1,0:T(8,128)(2,1)}, bf16[144,128]{1,0:T(8,128)(2,1)S(1)}, u32[]{:S(2)}, u32[]{:S(2)}) collective-permute-start(bf16[144,128]{1,0:T(8,128)(2,1)} %get-tuple-element.20), channel_id=1, source_target_pairs={{0,24},{8,16},{16,8},{24,0},{1,25},{9,17},{17,9},{25,1},{2,26},{10... | collective-permute-start | bytes 110600 | tf_op jit(solution)/shard_map/ppermute | solution.py:511
  11.5 0.8 copy-start.2
  12.3 0.7 copy-start.4
  14.7 31.2 %copy-start.10 = (f32[384]{0:T(512)S(1)}, f32[384]{0:T(512)}, u32[]{:S(2)}) copy-start(f32[384]{0:T(512)} %param.13) | copy-start | bytes 4612
  14.7 31.2 %copy-start.3 = (bf16[144,128]{1,0:T(8,128)(2,1)S(1)}, bf16[144,128]{1,0:T(8,128)(2,1)}, u32[]{:S(2)}) copy-start(bf16[144,128]{1,0:T(8,128)(2,1)} %get-tuple-element.17.refs_0_._) | copy-start | bytes 110596
  14.7 26.1 %all-to-all-start = ((bf16[8,160,128]{2,1,0:T(8,128)(2,1)}), bf16[8,160,128]{2,1,0:T(8,128)(2,1)S(1)}, u32[]{:S(2)}, u32[]{:S(2)}) async-start(bf16[8,160,128]{2,1,0:T(8,128)(2,1)} %slice_latents.1), calls=%async_computation | async-start | bytes 655360 | tf_op jit(solution)/shard_map/all_to_all | solution.py:517
  20.2 10.1 %collective-permute-start.3 = (bf16[1152,128]{1,0:T(8,128)(2,1)}, bf16[1152,128]{1,0:T(8,128)(2,1)S(1)}, u32[]{:S(2)}, u32[]{:S(2)}) collective-permute-start(bf16[1152,128]{1,0:T(8,128)(2,1)} %get-tuple-element.22), channel_id=1, source_target_pairs={{0,8},{8,0},{16,24},{24,16},{1,9},{9,1},{17,25},{25,17},{2,10},{10... | collective-permute-start | bytes 884744 | tf_op jit(solution)/shard_map/ppermute | solution.py:511
  20.7 14.5 %collective-permute-start.4 = (bf16[1152,128]{1,0:T(8,128)(2,1)}, bf16[1152,128]{1,0:T(8,128)(2,1)S(1)}, u32[]{:S(2)}, u32[]{:S(2)}) collective-permute-start(bf16[1152,128]{1,0:T(8,128)(2,1)} %get-tuple-element.23), channel_id=1, source_target_pairs={{0,16},{8,24},{16,0},{24,8},{1,17},{9,25},{17,1},{25,9},{2,18},{10... | collective-permute-start | bytes 884744 | tf_op jit(solution)/shard_map/ppermute | solution.py:511
  22.3 14.5 %collective-permute-start.5 = (bf16[1152,128]{1,0:T(8,128)(2,1)}, bf16[1152,128]{1,0:T(8,128)(2,1)S(1)}, u32[]{:S(2)}, u32[]{:S(2)}) collective-permute-start(bf16[1152,128]{1,0:T(8,128)(2,1)} %get-tuple-element.24), channel_id=1, source_target_pairs={{0,24},{8,16},{16,8},{24,0},{1,25},{9,17},{17,9},{25,1},{2,26},{10... | collective-permute-start | bytes 884744 | tf_op jit(solution)/shard_map/ppermute | solution.py:511
  36.7 1.0 copy-start.1
  37.7 0.7 copy-start.5
  40.8 74.3 %all-to-all-start.1 = ((bf16[8,1248,128]{2,1,0:T(8,128)(2,1)}), bf16[8,1248,128]{2,1,0:T(8,128)(2,1)S(1)}, u32[]{:S(2)}, u32[]{:S(2)}) async-start(bf16[8,1248,128]{2,1,0:T(8,128)(2,1)} %slice_caches.1), calls=%async_computation.1 | async-start | bytes 5111808 | tf_op jit(solution)/shard_map/all_to_all | solution.py:517
  45.9 9.6 %copy-start.6 = (s32[4,8]{1,0:T(4,128)S(1)}, s32[4,8]{1,0:T(4,128)}, u32[]{:S(2)}) copy-start(s32[4,8]{1,0:T(4,128)} %bands.7) | copy-start | bytes 388
  46.0 9.6 %copy-start.7 = (bf16[27,16,384]{2,1,0:T(8,128)(2,1)S(1)}, bf16[27,16,384]{2,1,0:T(8,128)(2,1)}, u32[]{:S(2)}) copy-start(bf16[27,16,384]{2,1,0:T(8,128)(2,1)} %win_ref.1) | copy-start | bytes 995332
  52.5 3.1 %copy-start = (bf16[3456,1152]{1,0:T(8,128)(2,1)}, bf16[3456,1152]{1,0:T(8,128)(2,1)S(1)}, u32[]{:S(2)}) copy-start(bf16[3456,1152]{1,0:T(8,128)(2,1)S(1)} %widen_weights.1.mid_ref.early_ref) | copy-start | bytes 23887876
  112.9 2.1 %copy-start.8 = (f32[96,2,16,384]{3,2,1,0:T(8,128)}, f32[96,2,16,384]{3,2,1,0:T(8,128)S(1)}, u32[]{:S(2)}) copy-start(f32[96,2,16,384]{3,2,1,0:T(8,128)S(1)} %get-tuple-element.27.part_in) | copy-start | bytes 14155780
  115.1 1.5 %copy-start.9 = (bf16[8,1248,128]{2,1,0:T(8,128)(2,1)}, bf16[8,1248,128]{2,1,0:T(8,128)(2,1)S(1)}, u32[]{:S(2)}) copy-start(bf16[8,1248,128]{2,1,0:T(8,128)(2,1)S(1)} %all-to-all-done.1) | copy-start | bytes 7667716
